TPU v7x, 512 devices: a whole 4x4x16 slice. The times are simulated.
512 devices in a mesh: span: 64 (over x, z), head: 8 (over y, core).
Axes of the slice: x: 4, y: 4, z: 16, core: 2. Of those that a mesh axis runs over, the one named last changes fastest.
Arguments:
- queries: bfloat16 [16384, 8192], P('span', 'head'), may hold values from -15 to 15
- keys: bfloat16 [16384, 1024], P(('span', 'head')), may hold values from -8 to 8
- values: bfloat16 [16384, 1024], P(('span', 'head')), may hold values from -6 to 6
- parent: int32 [32], replicated, may hold values from -1 to 15, as said below
- owner: int32 [32], replicated, may hold values from 0 to 31, each once
- lengths: int32 [32], replicated, may hold values from 1 to 512, as said below
Outputs:
- attended: bfloat16 [16384, 8192], P('span', 'head')
Inputs may be any that keep to these rules, and one draw needn't show every extreme that they name: Spans are numbered level by level from the roots down, with 4, 4, 8 and 16 spans on the four levels; a span's parent lies on the level above it, every span above the lowest level has a child, and no span has more than 3 ancestors. `owner`: each slot holds one span. `lengths`: every span that has a child holds 512 valid tokens; a span's valid tokens are its first ones.
All inputs are finite; a program needn't handle non-finite values.
Results may differ from a plain program's by a relative error of at most 0.0065.
Values may be sent and summed in bfloat16 or wider, within the bound.
No kernel may reach another device: no remote copies, remote signals or barrier semaphores. Data moves between devices by JAX's collectives and lax.ppermute only.
A program may use at most 64 MiB of HBM per device.

v0:
```python
from functools import reduce

import jax
import jax.numpy as jnp
from jax import lax
from jax.sharding import PartitionSpec as P

HD = 128


def shifted(shard, axis, by):
    size = lax.axis_size(axis)
    pairs = [(i, i + by) for i in range(size) if 0 <= i + by < size]
    return lax.ppermute(shard, axis, pairs)


def lookup(values_table, wanted_index):
    matches = wanted_index[..., None] == jnp.arange(values_table.shape[0], dtype=jnp.int32)
    return jnp.sum(jnp.where(matches, values_table, 0), axis=-1)


def ancestry(parent, owner, start_spans):
    lineage = []
    current = start_spans
    for height in range(3):
        upward = lookup(parent, jnp.maximum(current, 0))
        current = jnp.where(current >= 0, upward, -1)
        lineage.append((current >= 0, lookup(owner, jnp.maximum(current, 0))))
    return lineage


def on_device(queries, keys, values, parent, owner, lengths):
    devices = lax.axis_size("span")
    position = lax.axis_index("span")
    stacked = jnp.stack([keys, values])
    own_pair = lax.all_to_all(stacked, "head", split_axis=2, concat_axis=1, tiled=True)
    token_rows = own_pair.shape[1]
    kv_width = own_pair.shape[2]
    groups = kv_width // HD
    repeats = queries.shape[1] // kv_width
    query_head_total = queries.reshape(token_rows, groups, repeats, HD)
    scale_factor = HD ** (-0.5)
    device_ids = jnp.arange(devices, dtype=jnp.int32)
    span_ids = jnp.arange(owner.shape[0], dtype=jnp.int32)
    span_keepers = owner[None, :] == (device_ids // 2)[:, None]
    span_at = jnp.sum(jnp.where(span_keepers, span_ids[None, :], 0), axis=1)
    lineage = ancestry(parent, owner, span_at)
    is_mine = device_ids == position
    my_span = jnp.sum(jnp.where(is_mine, span_at, 0))

    def attend(running, key_block, allowed):
        maximum, weight_total, summed = running
        key_head_total = key_block[0].reshape(-1, groups, HD)
        value_heads = key_block[1].reshape(-1, groups, HD)
        scores = (
            jnp.einsum(
                "cnaw,xnw->nacx",
                query_head_total,
                key_head_total,
                preferred_element_type=jnp.float32,
            )
            * scale_factor
        )
        if allowed is not None:
            scores = jnp.where(allowed, scores, -jnp.inf)
        newest = jnp.maximum(maximum, jnp.max(scores, axis=-1))
        shrink = jnp.exp(maximum - newest)
        weights = jnp.exp(scores - newest[..., None])
        weight_total = weight_total * shrink + jnp.sum(weights, axis=-1)
        summed = summed * shrink[..., None] + jnp.einsum(
            "puhk,kpq->puhq",
            weights.astype(jnp.bfloat16),
            value_heads,
            preferred_element_type=jnp.float32,
        )
        return (newest, weight_total, summed)

    def attend_full(running, key_block):
        return attend(running, key_block, None)

    def unchanged(running, key_block):
        return running

    start_state = (
        jnp.full((groups, repeats, token_rows), -jnp.inf, jnp.float32),
        jnp.zeros((groups, repeats, token_rows), jnp.float32),
        jnp.zeros((groups, repeats, token_rows, HD), jnp.float32),
    )
    row_ids = jnp.arange(token_rows, dtype=jnp.int32)
    causal = row_ids[:, None] >= row_ids[None, :]
    running = attend(start_state, own_pair, causal)
    partner = shifted(own_pair, "span", 1)
    running = lax.cond(position % 2 == 1, attend_full, unchanged, running, partner)
    gathered_piece = lax.all_gather(own_pair, "span", axis=1, tiled=True)
    piece_rows = gathered_piece.shape[1]
    block_rows = min(piece_rows, token_rows)

    def advance(block_index, inner_state):
        block_start = block_index * block_rows
        key_block = lax.dynamic_slice_in_dim(
            gathered_piece, block_index * block_rows, block_rows, 1
        )
        source_slot = block_start // token_rows // 2
        hits = [
            jnp.any(is_mine & present_flag & (slot_table == source_slot))
            for present_flag, slot_table in lineage
        ]
        wanted = reduce(jnp.logical_or, hits)
        return lax.cond(wanted, attend_full, unchanged, inner_state, key_block)

    running = lax.fori_loop(0, piece_rows // block_rows, advance, running)
    maximum, weight_total, summed = running
    result = summed / weight_total[..., None]
    result = result.transpose(2, 0, 1, 3).reshape(token_rows, groups * repeats * HD)
    positions = position % 2 * token_rows + row_ids
    local_length = lookup(lengths, my_span)
    valid_rows = positions < local_length
    return jnp.where(valid_rows[:, None], result, 0.0).astype(jnp.bfloat16)


def solution(mesh):
    return jax.shard_map(
        on_device,
        mesh=mesh,
        in_specs=(
            P("span", "head"),
            P(("span", "head"), None),
            P(("span", "head"), None),
            P(),
            P(),
            P(),
        ),
        out_specs=P("span", "head"),
        check_vma=False,
    )
```

profile of v0, /device:TPU:40, one launch (start us, length us, event | category | flops | bytes accessed | tf_op | source)
XLA Modules:
  0.0 408.1 jit_solution(2990007691628120567)
XLA Ops:
  6.5 0.9 pad_maximum_fusion
  8.4 9.4 %all_to_all.18 = bf16[8,2,4096]{2,1,0:T(2,128)(2,1)S(1)} all-to-all(bf16[8,2,4096]{2,1,0:T(2,128)(2,1)S(1)} %reshape.207), channel_id=1, replica_groups=mesh['span'=64,'head'=8] {'head'}, dimensions={0} | all-to-all | bytes 262144 | tf_op jit(solution)/shard_map/all_to_all | solution.py:36
  18.1 1.0 copy.46
  19.3 1.0 copy.51
  20.4 0.7 select_reduce_fusion.7
  21.1 1.4 fusion.39
  23.6 3.8 collective-permute-start
  28.2 0.8 fusion.32
  29.0 2.7 collective-permute-done
  31.8 1.8 conditional.2
  32.6 1.0 fusion.3
  33.6 146.3 %all-gather.2.cloned.1.call-done = bf16[2,16384,128]{2,1,0:T(8,128)(2,1)} async-done(((bf16[2,256,128]{2,1,0:T(8,128)(2,1)}), bf16[2,16384,128]{2,1,0:T(8,128)(2,1)}) %all-gather.2.cloned.1.call-update) | async-done | bytes 8388624 | tf_op jit(solution)/shard_map/all_gather | solution.py:94
  179.9 219.8 %while.20 = (s32[]{:T(128)}, f32[1,8,256]{2,1,0:T(8,128)S(1)}, f32[1,8,256]{2,1,0:T(8,128)S(1)}, f32[1,8,256,128]{3,2,1,0:T(8,128)S(1)}, s32[64]{0:T(128)S(1)}, ...) while((s32[]{:T(128)}, f32[1,8,256]{2,1,0:T(8,128)S(1)}, ...), condition=%wide.region_23.24_spmd, body=%wide.region_15.23_spmd.sunk | while | flops 273160800 | bytes 9176660 | solution.py:111
  232.2 3.8 conditional.4
  232.2 1.5 bitcast_reduce_fusion.1
  233.7 1.8 fusion.19
  239.0 3.8 conditional.4
  239.0 1.5 bitcast_reduce_fusion.1
  240.6 1.8 fusion.19
  264.3 3.8 conditional.4
  264.4 1.5 bitcast_reduce_fusion.1
  265.9 1.8 fusion.19
  271.2 3.8 conditional.4
  271.2 1.5 bitcast_reduce_fusion.1
  272.8 1.8 fusion.19
  333.5 3.8 conditional.4
  333.5 1.5 bitcast_reduce_fusion.1
  335.1 1.8 fusion.19
  340.4 3.8 conditional.4
  340.4 1.5 bitcast_reduce_fusion.1
  341.9 1.8 fusion.19
  400.3 1.0 fusion.35
  (251 shorter events, 88.1 us)
Async XLA Ops:
  6.5 12.6 %copy-start = (bf16[256,1024]{1,0:T(8,128)(2,1)S(1)}, bf16[256,1024]{1,0:T(8,128)(2,1)}, u32[]{:S(2)}) copy-start(bf16[256,1024]{1,0:T(8,128)(2,1)} %param.12) | copy-start | bytes 1572868
  6.5 173.3 %all-gather.2.cloned.1.call-start = ((), (), s32[]{:S(2)}) async-start(), calls=%async_computation.1 | async-start | bytes 8519680 | tf_op jit(solution)/shard_map/all_gather | solution.py:94
  7.9 12.4 %copy-start.2 = (s32[32]{0:T(128)S(1)}, s32[32]{0:T(128)}, u32[]{:S(2)}) copy-start(s32[32]{0:T(128)} %param.16) | copy-start | bytes 388
  7.9 13.2 %copy-start.3 = (s32[32]{0:T(128)S(1)}, s32[32]{0:T(128)}, u32[]{:S(2)}) copy-start(s32[32]{0:T(128)} %param.17) | copy-start | bytes 388
  7.9 15.2 %copy-start.4 = (s32[32]{0:T(128)S(1)}, s32[32]{0:T(128)}, u32[]{:S(2)}) copy-start(s32[32]{0:T(128)} %param.15) | copy-start | bytes 388
  19.0 4.5 %copy-start.1 = (bf16[2,32,8,128]{3,1,2,0:T(8,128)(2,1)S(1)}, bf16[2,32,8,128]{3,1,2,0:T(8,128)(2,1)}, u32[]{:S(2)}) copy-start(bf16[2,32,8,128]{3,1,2,0:T(8,128)(2,1)} %copy.46) | copy-start | bytes 393220
  23.6 8.2 %collective-permute-start = (bf16[2,256,128]{2,1,0:T(8,128)(2,1)S(1)}, bf16[2,256,128]{2,1,0:T(8,128)(2,1)S(1)}, u32[]{:S(2)}, u32[]{:S(2)}) collective-permute-start(bf16[2,256,128]{2,1,0:T(8,128)(2,1)S(1)} %bitcast.148), channel_id=1, source_target_pairs={{0,8},{8,16},{16,24},{24,32},{32,40},{40,48},{48,56},{56,64},{64,7... | collective-permute-start | bytes 393224 | tf_op jit(solution)/shard_map/ppermute | solution.py:14
Sparse Core Ops, SparseCore 0:
  19.2 160.6 all-gather.1
where the time goes:
time: 411 us; the launch traced here: 408 us
  waiting for transfers between devices  149 us (36%)
  loops' own time  117 us (28%)
  other arithmetic  88.6 us (22%)
  matrix products  22.6 us (5%)
  between operations  13.6 us (3%)
  blocking collectives  9.39 us (2%)
    all_gather x1, waiting for transfers between devices, on_device(): gathered_piece = lax.all_gather(own_pair, 'span', axis=1, tiled=True)  146 us
    another operation x1, loops' own time, on_device(): running = lax.fori_loop(0, piece_rows // block_rows, advance, running)  116 us
    reduce_or x128, other arithmetic, advance(): jnp.any(is_mine & present_flag & (slot_table == source_slot))  80.2 us
    dot_general x8, matrix products, attend(): jnp.einsum('puhk,kpq->puhq', weights.astype(jnp.bfloat16), value_heads, p...  12.6 us
    dot_general x8, matrix products, attend(): jnp.einsum('cnaw,xnw->nacx', query_head_total, key_head_total, preferred_...  10 us
    all_to_all x1, blocking collectives, on_device(): lax.all_to_all(stacked, 'head', split_axis=2, concat_axis=1, tiled=True)  9.39 us
  transfers between devices with their start and end apart: 2, of which 2 were waited for; matrix products, arithmetic and copies ran while one was open for 2% of the time, Pallas kernels for 0%

commit v1 on v0

v1 whole, which is shorter than its diff:
```python
import functools

import jax
import jax.numpy as jnp
from jax import lax
from jax.experimental import pallas as pl
from jax.experimental.pallas import tpu as pltpu
from jax.sharding import Mesh, PartitionSpec as P

HD = 128
HEADS = 8
HALF = 256
CHUNK = 32
PIECE = 16
SLOTS = 32
LEVELS = 3
EXP_FACTOR = HD ** (-0.5) * 1.4426950408889634

VMEM = pl.BlockSpec(memory_space=pltpu.VMEM)
SMEM = pl.BlockSpec(memory_space=pltpu.SMEM)


def pack_kernel(keys_ref, values_ref, out_ref):
    for head in range(HEADS):
        columns = pl.ds(head * HD, HD)
        for kind, ref in enumerate((keys_ref, values_ref)):
            block = ref[:, columns]
            out_ref[head, kind] = block
            out_ref[HEADS + head, kind] = block


def split_kernel(own_ref, out_ref):
    half = lax.axis_index("zl")
    for head in range(HEADS):
        for kind in range(2):
            block = own_ref[half * HEADS + head, kind]
            first = kind * (HALF // PIECE) + head * 2
            out_ref[pl.ds(first, 2)] = block.reshape(2, PIECE, HD)


def pick_kernel(parent_ref, owner_ref, spread_ref, out_ref, span_at_ref):
    for span in range(SLOTS):
        span_at_ref[owner_ref[span]] = span
    for slot in range(SLOTS):
        current = span_at_ref[slot]
        for level in range(LEVELS):
            current = jnp.where(current >= 0, parent_ref[jnp.maximum(current, 0)], -1)
            source = owner_ref[jnp.maximum(current, 0)]
            out_ref[slot, level] = spread_ref[source]


def attend_kernel(parent_ref, owner_ref, lengths_ref, queries_ref, own_ref, near_ref, far_ref, out_ref):
    half = lax.axis_index("zl")
    my_slot = lax.axis_index("x") * 8 + lax.axis_index("zh")
    my_span = jnp.int32(0)
    for span in range(SLOTS):
        my_span = jnp.where(owner_ref[span] == my_slot, span, my_span)
    local_length = lengths_ref[my_span]
    count = jnp.int32(0)
    current = my_span
    for _ in range(LEVELS):
        current = jnp.where(current >= 0, parent_ref[jnp.maximum(current, 0)], -1)
        count = count + jnp.where(current >= 0, 1, 0)

    row_ids = lax.broadcasted_iota(jnp.int32, (HALF, HALF), 0)
    column_ids = lax.broadcasted_iota(jnp.int32, (HALF, HALF), 1)

    def own_rows(which, kind):
        return own_ref[pl.ds(which * HEADS, HEADS), kind].reshape(HALF, HD)

    def piece_rows(ref, level, kind):
        return ref[pl.ds(kind * 16, 16), level].reshape(HALF, HD)

    def body(levels, second):
        def key_blocks(kind):
            if second:
                yield own_rows(1, kind)
                yield own_rows(0, kind)
            else:
                yield own_rows(0, kind)
            for level in range(levels):
                yield piece_rows(near_ref, level, kind)
                yield piece_rows(far_ref, level, kind)

        def one_head(head, carry):
            columns = pl.ds(pl.multiple_of(head * HD, HD), HD)
            query = queries_ref[:, columns]
            scores = []
            for index, block in enumerate(key_blocks(0)):
                part = lax.dot_general(
                    query, block, (((1,), (1,)), ((), ())), preferred_element_type=jnp.float32
                )
                if index == 0:
                    part = jnp.where(row_ids >= column_ids, part, -jnp.inf)
                scores.append(part)
            top = functools.reduce(jnp.maximum, scores)
            top = jnp.max(top, axis=1, keepdims=True)
            total = None
            summed = None
            for part, block in zip(scores, key_blocks(1)):
                weights = jnp.exp2((part - top) * EXP_FACTOR)
                total = weights if total is None else total + weights
                product = jnp.dot(
                    weights.astype(jnp.bfloat16), block, preferred_element_type=jnp.float32
                )
                summed = product if summed is None else summed + product
            total = jnp.sum(total, axis=1, keepdims=True)
            result = summed / total
            positions = half * HALF + lax.broadcasted_iota(jnp.int32, (HALF, HD), 0)
            result = jnp.where(positions < local_length, result, 0.0)
            out_ref[:, columns] = result.astype(jnp.bfloat16)
            return carry

        lax.fori_loop(0, HEADS, one_head, 0)

    for levels in range(LEVELS + 1):
        for second in (False, True):

            @pl.when((count == levels) & (half == (1 if second else 0)))
            def _(levels=levels, second=second):
                body(levels, second)


def on_device(queries, keys, values, parent, owner, lengths):
    bf16 = jnp.bfloat16
    packed = pl.pallas_call(
        pack_kernel,
        out_shape=jax.ShapeDtypeStruct((16, 2, CHUNK, HD), bf16),
        in_specs=[VMEM, VMEM],
        out_specs=VMEM,
        name="pack_heads",
    )(keys, values)
    own = lax.all_to_all(packed, ("zl", "y", "c"), 0, 0, tiled=True)
    pieces = pl.pallas_call(
        split_kernel,
        out_shape=jax.ShapeDtypeStruct((SLOTS, PIECE, HD), bf16),
        in_specs=[VMEM],
        out_specs=VMEM,
        name="split_half",
    )(own)
    spread = lax.all_to_all(pieces, ("x", "zh"), 0, 0, tiled=True)
    picked = pl.pallas_call(
        pick_kernel,
        out_shape=jax.ShapeDtypeStruct((SLOTS, LEVELS, PIECE, HD), bf16),
        in_specs=[SMEM, SMEM, VMEM],
        out_specs=VMEM,
        scratch_shapes=[pltpu.SMEM((SLOTS,), jnp.int32)],
        name="pick_ancestors",
    )(parent, owner, spread)
    near = lax.all_to_all(picked, ("x", "zh"), 0, 0, tiled=True)
    far = lax.ppermute(near, "zl", [(0, 1), (1, 0)])
    return pl.pallas_call(
        attend_kernel,
        out_shape=jax.ShapeDtypeStruct((HALF, HEADS * HD), bf16),
        in_specs=[SMEM, SMEM, SMEM, VMEM, VMEM, VMEM, VMEM],
        out_specs=VMEM,
        compiler_params=pltpu.CompilerParams(vmem_limit_bytes=32 * 1024 * 1024),
        name="attend",
    )(parent, owner, lengths, queries, own, near, far)


def solution(mesh):
    fine = Mesh(mesh.devices.reshape(4, 8, 2, 4, 2), ("x", "zh", "zl", "y", "c"))
    span, head = ("x", "zh", "zl"), ("y", "c")
    return jax.shard_map(
        on_device,
        mesh=fine,
        in_specs=(P(span, head), P(span + head, None), P(span + head, None), P(), P(), P()),
        out_specs=P(span, head),
        check_vma=False,
    )
```

time: 411 us -> 105 us (0.26)
  the two profiles are of different devices: /device:TPU:40 before, /device:TPU:70 now
where the time goes in v1:
time: 105 us
  blocking collectives  77.7 us (74%)
  Pallas kernels  14.9 us (14%)
  waiting for transfers between devices  10.4 us (10%)
  starting transfers between devices  1.91 us (2%)
    all_to_all x1, blocking collectives, on_device(): near = lax.all_to_all(picked, ('x', 'zh'), 0, 0, tiled=True)  32.7 us
    all_to_all x1, blocking collectives, on_device(): spread = lax.all_to_all(pieces, ('x', 'zh'), 0, 0, tiled=True)  30.9 us
    all_to_all x1, blocking collectives, on_device(): own = lax.all_to_all(packed, ('zl', 'y', 'c'), 0, 0, tiled=True)  14.1 us
    ppermute x1, waiting for transfers between devices, on_device(): far = lax.ppermute(near, 'zl', [(0, 1), (1, 0)])  10.4 us
    pallas_call x1, Pallas kernels, on_device(): pl.pallas_call(attend_kernel, out_shape=jax.ShapeDtypeStruct((HALF, HEADS...  9.71 us
  transfers between devices with their start and end apart: 1, of which 1 were waited for; matrix products, arithmetic and copies ran while one was open for 0% of the time, Pallas kernels for 0%

profile of v1, /device:TPU:70, one launch (start us, length us, event | category | flops | bytes accessed | tf_op | source)
XLA Modules:
  0.0 105.0 jit_solution(11693998053603944222)
XLA Ops:
  0.0 1.6 %pack_heads.1 = bf16[16,2,32,128]{3,2,1,0:T(8,128)(2,1)} custom-call(bf16[32,1024]{1,0:T(8,128)(2,1)} %keys_ref.1, bf16[32,1024]{1,0:T(8,128)(2,1)} %values_ref.1), custom_call_target="tpu_custom_call" | custom-call | tf_op jit(solution)/shard_map/pack_heads/pallas_call | solution.py:126
  1.6 14.1 %all_to_all.15.own_ref = bf16[16,2,32,128]{3,2,1,0:T(8,128)(2,1)} all-to-all(bf16[16,2,32,128]{3,2,1,0:T(8,128)(2,1)} %pack_heads.1), channel_id=1, replica_groups=mesh['x'=4,'zh'=8,'zl'=2,'y'=4,'c'=2] {'zl','y','c'}, dimensions={0} | all-to-all | bytes 524288 | tf_op jit(solution)/shard_map/all_to_all | solution.py:133
  15.7 1.6 %split_half.1 = bf16[32,16,128]{2,1,0:T(8,128)(2,1)} custom-call(bf16[16,2,32,128]{3,2,1,0:T(8,128)(2,1)} %all_to_all.15.own_ref), custom_call_target="tpu_custom_call" | custom-call | tf_op jit(solution)/shard_map/split_half/pallas_call | solution.py:134
  17.3 30.9 %all_to_all.16.spread_ref = bf16[32,16,128]{2,1,0:T(8,128)(2,1)} all-to-all(bf16[32,16,128]{2,1,0:T(8,128)(2,1)} %split_half.1), channel_id=1, replica_groups=mesh['x'=4,'zh'=8,'zl'=2,'y'=4,'c'=2] {'x','zh'}, dimensions={0} | all-to-all | bytes 262144 | tf_op jit(solution)/shard_map/all_to_all | solution.py:141
  48.2 0.0 copy-start.2
  48.2 0.0 copy-start.3
  48.2 0.0 copy-start.4
  48.2 2.0 %pick_ancestors.1 = bf16[32,3,16,128]{3,2,1,0:T(8,128)(2,1)} custom-call(s32[32]{0:T(128)} %parent_ref.3, s32[32]{0:T(128)} %owner_ref.3, bf16[32,16,128]{2,1,0:T(8,128)(2,1)} %all_to_all.16.spread_ref), custom_call_target="tpu_custom_call" | custom-call | tf_op jit(solution)/shard_map/pick_ancestors/pallas_call | solution.py:142
  50.2 0.0 copy-start
  50.2 0.0 copy-start.1
  50.2 32.7 %all_to_all.17.near_ref = bf16[32,3,16,128]{3,2,1,0:T(8,128)(2,1)S(1)} all-to-all(bf16[32,3,16,128]{3,2,1,0:T(8,128)(2,1)} %pick_ancestors.1), channel_id=1, replica_groups=mesh['x'=4,'zh'=8,'zl'=2,'y'=4,'c'=2] {'x','zh'}, dimensions={0} | all-to-all | bytes 786432 | tf_op jit(solution)/shard_map/all_to_all | solution.py:150
  82.9 1.9 %collective-permute-start = (bf16[32,3,16,128]{3,2,1,0:T(8,128)(2,1)S(1)}, bf16[32,3,16,128]{3,2,1,0:T(8,128)(2,1)S(1)}, u32[]{:S(2)}, u32[]{:S(2)}) collective-permute-start(bf16[32,3,16,128]{3,2,1,0:T(8,128)(2,1)S(1)} %all_to_all.17.near_ref), channel_id=1, source_target_pairs={{0,8},{8,0},{1,9},{9,1},{2,10},{10,2},{3,11},{11,3},{4,12},{12,4},... | collective-permute-start | bytes 1179656 | tf_op jit(solution)/shard_map/ppermute | solution.py:151
  84.8 10.4 %collective-permute-done.far_ref = bf16[32,3,16,128]{3,2,1,0:T(8,128)(2,1)S(1)} collective-permute-done((bf16[32,3,16,128]{3,2,1,0:T(8,128)(2,1)S(1)}, bf16[32,3,16,128]{3,2,1,0:T(8,128)(2,1)S(1)}, u32[]{:S(2)}, u32[]{:S(2)}) %collective-permute-start) | collective-permute-done | bytes 393248 | tf_op jit(solution)/shard_map/ppermute | solution.py:151
  95.3 0.0 copy-done.2
  95.3 0.0 copy-done.3
  95.3 0.0 copy-done.4
  95.3 0.0 copy-done
  95.3 0.0 copy-done.1
  95.3 9.7 %attend.1 = bf16[256,1024]{1,0:T(8,128)(2,1)} custom-call(s32[32]{0:T(128)S(1)} %copy-done.2, s32[32]{0:T(128)S(1)} %copy-done.3, s32[32]{0:T(128)S(1)} %copy-done.4, bf16[256,1024]{1,0:T(8,128)(2,1)S(1)} %copy-done.1, bf16[16,2,32,128]{3,2,1,0:T(8,128)(2,1)S(1)} %copy-done, bf16[32,3,16,128]{3,2,1,0:T(8,128)(2,1)S(1)} %all_to_all.17.near_ref, ...), custom_call_target="tpu_custom_call" | custom-call | tf_op jit(solution)/shard_map/attend/pallas_call | solution.py:152
Async XLA Ops:
  48.2 47.1 %copy-start.2 = (s32[32]{0:T(128)S(1)}, s32[32]{0:T(128)}, u32[]{:S(2)}) copy-start(s32[32]{0:T(128)} %parent_ref.3) | copy-start | bytes 388
  48.2 47.1 %copy-start.3 = (s32[32]{0:T(128)S(1)}, s32[32]{0:T(128)}, u32[]{:S(2)}) copy-start(s32[32]{0:T(128)} %owner_ref.3) | copy-start | bytes 388
  48.2 47.1 %copy-start.4 = (s32[32]{0:T(128)S(1)}, s32[32]{0:T(128)}, u32[]{:S(2)}) copy-start(s32[32]{0:T(128)} %lengths_ref.1) | copy-start | bytes 388
  50.2 45.1 %copy-start = (bf16[16,2,32,128]{3,2,1,0:T(8,128)(2,1)S(1)}, bf16[16,2,32,128]{3,2,1,0:T(8,128)(2,1)}, u32[]{:S(2)}) copy-start(bf16[16,2,32,128]{3,2,1,0:T(8,128)(2,1)} %all_to_all.15.own_ref) | copy-start | bytes 786436
  50.2 45.1 %copy-start.1 = (bf16[256,1024]{1,0:T(8,128)(2,1)S(1)}, bf16[256,1024]{1,0:T(8,128)(2,1)}, u32[]{:S(2)}) copy-start(bf16[256,1024]{1,0:T(8,128)(2,1)} %queries_ref.1) | copy-start | bytes 1572868
  82.9 12.4 %collective-permute-start = (bf16[32,3,16,128]{3,2,1,0:T(8,128)(2,1)S(1)}, bf16[32,3,16,128]{3,2,1,0:T(8,128)(2,1)S(1)}, u32[]{:S(2)}, u32[]{:S(2)}) collective-permute-start(bf16[32,3,16,128]{3,2,1,0:T(8,128)(2,1)S(1)} %all_to_all.17.near_ref), channel_id=1, source_target_pairs={{0,8},{8,0},{1,9},{9,1},{2,10},{10,2},{3,11},{11,3},{4,12},{12,4},... | collective-permute-start | bytes 1179656 | tf_op jit(solution)/shard_map/ppermute | solution.py:151

commit v2 on v1

v2 whole, which is shorter than its diff:
```python
import functools

import jax
import jax.numpy as jnp
from jax import lax
from jax.experimental import pallas as pl
from jax.experimental.pallas import tpu as pltpu
from jax.sharding import Mesh, PartitionSpec as P

HD = 128
HEADS = 8
HALF = 256
SPANS = 32
LEVELS = 3
PLACES = 8
STRIP = 8
SHARE = HEADS * STRIP
TABLE = 8
ROW = 128
HIDDEN = -1e30
EXP_FACTOR = HD ** (-0.5) * 1.4426950408889634

VMEM = pl.BlockSpec(memory_space=pltpu.VMEM)
SMEM = pl.BlockSpec(memory_space=pltpu.SMEM)


def pack_kernel(parent_ref, owner_ref, lengths_ref, keys_ref, values_ref, out_ref, facts_ref, span_at_ref):
    for kind, ref in enumerate((keys_ref, values_ref)):
        for strip in range(4):
            rows = ref[pl.ds(strip * STRIP, STRIP), :]
            for head in range(HEADS):
                columns = rows[:, head * HD : (head + 1) * HD]
                out_ref[kind * 2 + strip // 2, strip % 2, pl.ds(head * STRIP, STRIP), :] = columns
    half = lax.axis_index("zl")
    pair = lax.axis_index("zb") * 2 + lax.axis_index("i")
    mine = lax.axis_index("x")
    beside = (pair + 7 + half * 2) & 7
    for span in range(SPANS):
        span_at_ref[owner_ref[span]] = span
    my_count = jnp.int32(0)
    my_length = jnp.int32(0)
    for x in range(4):
        for side in range(2):
            slot = x * 8 + (pair if side == 0 else beside)
            current = span_at_ref[slot]
            length = lengths_ref[current]
            count = jnp.int32(0)
            entry = TABLE + (x * 2 + side) * (1 + LEVELS)
            facts_ref[entry] = ((slot >> 1) & 3) * PLACES + (slot >> 3) * 2 + (slot & 1)
            for level in range(LEVELS):
                current = jnp.where(current >= 0, parent_ref[jnp.maximum(current, 0)], -1)
                count = count + jnp.where(current >= 0, 1, 0)
                slot = owner_ref[jnp.maximum(current, 0)]
                facts_ref[entry + 1 + level] = ((slot >> 1) & 3) * PLACES + (slot >> 3) * 2 + (slot & 1)
            if side == 0:
                my_count = jnp.where(mine == x, count, my_count)
                my_length = jnp.where(mine == x, length, my_length)
    facts_ref[0] = my_count
    facts_ref[1] = my_length


def pick_kernel(facts_ref, gathered_ref, out_ref):
    for x in range(4):
        for side in range(2):
            for level in range(1 + LEVELS):
                source = facts_ref[TABLE + (x * 2 + side) * (1 + LEVELS) + level]
                out_ref[x, side, level] = gathered_ref[source]


def partial_attention(queries, keys, values, causal):
    all_scores = [
        lax.dot_general(keys, query, (((1,), (1,)), ((), ())), preferred_element_type=jnp.float32)
        for query in queries
    ]
    for scores in all_scores:
        if causal is not None:
            masked = jnp.where(causal, scores[:ROW], HIDDEN)
            scores = jnp.concatenate([masked, scores[ROW:]], axis=0) if scores.shape[0] > ROW else masked
        top = jnp.max(scores, axis=0, keepdims=True)
        weights = jnp.exp2((scores - top) * EXP_FACTOR)
        total = jnp.sum(weights, axis=0, keepdims=True)
        summed = lax.dot_general(
            values, weights.astype(jnp.bfloat16), (((0,), (0,)), ((), ())), preferred_element_type=jnp.float32
        )
        yield top, total, summed


def save(summed_ref, stats_ref, head, top, total, summed):
    summed_ref[head] = summed
    stats_ref[head, pl.ds(0, 8)] = jnp.broadcast_to(top, (8, HALF))
    stats_ref[head, pl.ds(8, 8)] = jnp.broadcast_to(total, (8, HALF))


def head_queries(queries_ref):
    return [queries_ref[:, head * HD : (head + 1) * HD] for head in range(HEADS)]


def chunk_rows(ref, kind, with_own, levels):
    blocks = []
    if with_own:
        blocks.append(ref[pl.ds(kind * 2, 2), 0].reshape(ROW, HD))
    if levels > 0:
        blocks.append(ref[pl.ds(kind * 2, 2), 1 : 1 + levels].reshape(levels * ROW, HD))
    return blocks


def causal_mask(source_i):
    rows = lax.broadcasted_iota(jnp.int32, (ROW, HALF), 1)
    spots = lax.broadcasted_iota(jnp.int32, (ROW, HALF), 0)
    key_rows = ((spots & 56) << 2) + ((spots >> 6) << 4) + (spots & 7)
    return rows >= key_rows + source_i * STRIP


def attend_kernel(begins, ends, near_count, far_count, facts_ref, queries_ref, *refs):
    chunk_count = near_count + far_count
    chunks, rest = refs[:chunk_count], refs[chunk_count:]
    state, outs = ((), rest) if begins else (rest[:2], rest[2:])
    half = lax.axis_index("zl")
    own_i = lax.axis_index("i")
    count = facts_ref[0]
    causal = causal_mask(own_i if begins else 1 - own_i) if near_count else None
    positions = half * HALF + lax.broadcasted_iota(jnp.int32, (HALF, HD), 0)
    valid = positions < facts_ref[1]

    def finish(head, top, total, summed):
        if ends:
            result = (summed * (1.0 / total)).T
            outs[0][:, head * HD : (head + 1) * HD] = jnp.where(valid, result, 0.0).astype(jnp.bfloat16)
        else:
            save(*outs, head, top, total, summed)

    def stored(head):
        return state[1][head, pl.ds(0, 8)][:1], state[1][head, pl.ds(8, 8)][:1], state[0][head]

    def body(levels, second):
        def rows_of(kind):
            blocks = []
            for index, chunk in enumerate(chunks):
                blocks += chunk_rows(chunk, kind, index < near_count or second, levels)
            return blocks

        if not rows_of(0):
            for head in range(HEADS):
                finish(head, *stored(head))
            return
        keys, values = (jnp.concatenate(rows_of(kind), axis=0) for kind in range(2))
        parts = partial_attention(head_queries(queries_ref), keys, values, causal)
        for head, (top2, total2, summed2) in enumerate(parts):
            if begins:
                finish(head, top2, total2, summed2)
                continue
            top, total, summed = stored(head)
            newest = jnp.maximum(top, top2)
            shrink = jnp.exp2((top - newest) * EXP_FACTOR)
            shrink2 = jnp.exp2((top2 - newest) * EXP_FACTOR)
            finish(head, newest, total * shrink + total2 * shrink2, summed * shrink + summed2 * shrink2)

    for levels in range(LEVELS + 1):
        if far_count == 0:
            pl.when(count == levels)(functools.partial(body, levels, False))
            continue
        for second in (False, True):
            here = (count == levels) & (half == (1 if second else 0))
            pl.when(here)(functools.partial(body, levels, second))


def on_device(queries, keys, values, parent, owner, lengths):
    bf16, f32 = jnp.bfloat16, jnp.float32
    params = pltpu.CompilerParams(vmem_limit_bytes=32 * 1024 * 1024)
    work = pl.CostEstimate(
        flops=4 * HEADS * HALF * HD * 1024, bytes_accessed=4 * 1024 * 1024, transcendentals=HEADS * HALF * 1024
    )
    small = pltpu.CompilerParams(vmem_limit_bytes=4 * 1024 * 1024)
    packed, facts = pl.pallas_call(
        pack_kernel,
        out_shape=[
            jax.ShapeDtypeStruct((4, 2, SHARE, HD), bf16),
            jax.ShapeDtypeStruct((TABLE + PLACES * (1 + LEVELS),), jnp.int32),
        ],
        in_specs=[SMEM, SMEM, SMEM, VMEM, VMEM],
        out_specs=[VMEM, SMEM],
        scratch_shapes=[pltpu.SMEM((SPANS,), jnp.int32)],
        name="pack_heads",
    )(parent, owner, lengths, keys, values)
    spread = lax.all_to_all(packed.reshape(64, STRIP, HD), ("x", "i", "y", "c"), 0, 0, tiled=True)
    gathered = lax.all_gather(spread.reshape(PLACES, SHARE, HD), "zb", axis=0, tiled=True)
    picked = pl.pallas_call(
        pick_kernel,
        out_shape=jax.ShapeDtypeStruct((4, 2, 1 + LEVELS, SHARE, HD), bf16),
        in_specs=[SMEM, VMEM],
        out_specs=VMEM,
        compiler_params=small,
        name="pick_ancestors",
    )(facts, gathered)
    passed = lax.all_to_all(picked, "x", 0, 0, tiled=True)
    ours, beside = passed[:, 0], passed[:, 1]
    ring = ("zb", "i", "zl")
    far = lax.ppermute(ours, ring, [(z, z ^ 1) for z in range(16)])
    further = lax.ppermute(beside, ring, [(z, (z + (1 if z % 2 else -1)) % 16) for z in range(16)])
    state = [jax.ShapeDtypeStruct((HEADS, HD, HALF), f32), jax.ShapeDtypeStruct((HEADS, 16, HALF), f32)]

    def attend(name, begins, ends, near_count, far_count, *operands):
        return pl.pallas_call(
            functools.partial(attend_kernel, begins, ends, near_count, far_count),
            out_shape=jax.ShapeDtypeStruct((HALF, HEADS * HD), bf16) if ends else state,
            in_specs=[SMEM] + [VMEM] * (1 + len(operands)),
            out_specs=VMEM if ends else [VMEM, VMEM],
            compiler_params=params,
            cost_estimate=work,
            name=name,
        )(facts, queries, *operands)

    running = attend("attend_own", True, False, 1, 0, ours)
    beside, running = lax.optimization_barrier((beside, running))
    near = lax.ppermute(beside, ring, [(z, (z + (2 if z % 2 else -2)) % 16) for z in range(16)])
    running = attend("attend_middle", False, False, 0, 2, far, further, *running)
    return attend("attend_last", False, True, 1, 0, near, *running)


def solution(mesh):
    fine = Mesh(mesh.devices.reshape(4, 4, 2, 2, 4, 2), ("x", "zb", "i", "zl", "y", "c"))
    span, head = ("x", "zb", "i", "zl"), ("y", "c")
    return jax.shard_map(
        on_device,
        mesh=fine,
        in_specs=(P(span, head), P(span + head, None), P(span + head, None), P(), P(), P()),
        out_specs=P(span, head),
        check_vma=False,
    )
```

time: 105 us -> 89.6 us (0.85)
  the two profiles are of different devices: /device:TPU:70 before, /device:TPU:72 now
where the time goes in v2:
time: 89.6 us; the launch traced here: 89.3 us
  blocking collectives  57.6 us (64%)
  starting transfers between devices  14.5 us (16%)
  Pallas kernels  10.7 us (12%)
  waiting for transfers between devices  5.72 us (6%)
    all_gather x1, blocking collectives, on_device(): lax.all_gather(spread.reshape(PLACES, SHARE, HD), 'zb', axis=0, tiled=True)  26.3 us
    all_to_all x1, blocking collectives, on_device(): lax.all_to_all(packed.reshape(64, STRIP, HD), ('x', 'i', 'y', 'c'), 0, 0,...  16.4 us
    all_to_all x1, blocking collectives, on_device(): passed = lax.all_to_all(picked, 'x', 0, 0, tiled=True)  14.8 us
    pallas_call x3, Pallas kernels, attend(): pl.pallas_call(functools.partial(attend_kernel, begins, ends, near_count,...  8.52 us
    ppermute x1, starting transfers between devices, on_device(): far = lax.ppermute(ours, ring, [(z, z ^ 1) for z in range(16)])  6.38 us
    ppermute x1, starting transfers between devices, on_device(): lax.ppermute(beside, ring, [(z, (z + (1 if z % 2 else -1)) % 16) for z in...  6.22 us
    ppermute x1, waiting for transfers between devices, on_device(): lax.ppermute(beside, ring, [(z, (z + (2 if z % 2 else -2)) % 16) for z in...  4.13 us
    ppermute x1, starting transfers between devices, on_device(): lax.ppermute(beside, ring, [(z, (z + (2 if z % 2 else -2)) % 16) for z in...  1.92 us
  transfers between devices with their start and end apart: 3, of which 2 were waited for; matrix products, arithmetic and copies ran while one was open for 0% of the time, Pallas kernels for 6%

profile of v2, /device:TPU:72, one launch (start us, length us, event | category | flops | bytes accessed | tf_op | source)
XLA Modules:
  0.0 89.3 jit_solution(7152457278557143306)
XLA Ops:
  0.0 1.6 %pack_heads.1 = (bf16[4,2,64,128]{3,2,1,0:T(8,128)(2,1)}, s32[40]{0:T(128)}) custom-call(s32[32]{0:T(128)} %parent_ref.1, s32[32]{0:T(128)} %owner_ref.1, s32[32]{0:T(128)} %lengths_ref.1, bf16[32,1024]{1,0:T(8,128)(2,1)} %keys_ref.1, bf16[32,1024]{1,0:T(8,128)(2,1)} %values_ref.1), custom_call_target="tpu_custom_call" | custom-call | tf_op jit(solution)/shard_map/pack_heads/pallas_call | solution.py:174
  1.6 16.4 %all_to_all.10 = bf16[64,8,128]{2,1,0:T(8,128)(2,1)S(1)} all-to-all(bf16[64,8,128]{2,1,0:T(8,128)(2,1)} %bitcast.11), channel_id=1, replica_groups=mesh['x'=4,'zb'=4,'i'=2,'zl'=2,'y'=4,'c'=2] {'x','i','y','c'}, dimensions={0} | all-to-all | bytes 262144 | tf_op jit(solution)/shard_map/all_to_all | solution.py:185
  18.1 26.3 %all_gather.3.gathered_ref = bf16[32,64,128]{2,1,0:T(8,128)(2,1)S(1)} all-gather(bf16[8,64,128]{2,1,0:T(8,128)(2,1)S(1)} %bitcast.10), channel_id=1, replica_groups=mesh['x'=4,'zb'=4,'i'=2,'zl'=2,'y'=4,'c'=2] {'zb'}, dimensions={0}, use_global_device_ids=true | all-gather | bytes 655360 | tf_op jit(solution)/shard_map/all_gather | solution.py:186
  44.4 0.0 copy-start
  44.4 0.7 copy-done
  45.1 0.6 pick_ancestors.1
  45.7 14.8 %all_to_all.11 = bf16[4,2,4,64,128]{4,3,2,1,0:T(8,128)(2,1)S(1)} all-to-all(bf16[4,2,4,64,128]{4,3,2,1,0:T(8,128)(2,1)S(1)} %pick_ancestors.1), channel_id=1, replica_groups=mesh['x'=4,'zb'=4,'i'=2,'zl'=2,'y'=4,'c'=2] {'x'}, dimensions={0} | all-to-all | bytes 1048576 | tf_op jit(solution)/shard_map/all_to_all | solution.py:195
  60.4 0.0 copy-start.1
  60.5 6.4 %collective-permute-start.1 = (bf16[4,4,64,128]{3,2,1,0:T(8,128)(2,1)S(1)}, bf16[4,4,64,128]{3,2,1,0:T(8,128)(2,1)S(1)}, u32[]{:S(2)}, u32[]{:S(2)}) collective-permute-start(bf16[4,4,64,128]{3,2,1,0:T(8,128)(2,1)S(1)} %get-tuple-element.23.refs_0_), channel_id=1, source_target_pairs={{0,8},{8,0},{16,24},{24,16},{32,40},{40,32},{48,56},{56,48},{64,72... | collective-permute-start | bytes 786440 | tf_op jit(solution)/shard_map/ppermute | solution.py:198
  66.9 6.2 %collective-permute-start.2 = (bf16[4,4,64,128]{3,2,1,0:T(8,128)(2,1)S(1)}, bf16[4,4,64,128]{3,2,1,0:T(8,128)(2,1)S(1)}, u32[]{:S(2)}, u32[]{:S(2)}) collective-permute-start(bf16[4,4,64,128]{3,2,1,0:T(8,128)(2,1)S(1)} %get-tuple-element.18), channel_id=1, source_target_pairs={{0,120},{8,16},{16,8},{24,32},{32,24},{40,48},{48,40},{56,64},{64,... | collective-permute-start | bytes 786440 | tf_op jit(solution)/shard_map/ppermute | solution.py:199
  73.1 0.0 copy-done.1
  73.1 2.3 %attend_own.1 = (f32[8,128,256]{2,1,0:T(8,128)S(1)}, f32[8,16,256]{2,1,0:T(8,128)S(1)}) custom-call(s32[40]{0:T(128)S(1)} %copy-done, bf16[256,1024]{1,0:T(8,128)(2,1)S(1)} %copy-done.1, bf16[4,4,64,128]{3,2,1,0:T(8,128)(2,1)S(1)} %get-tuple-element.23.refs_0_), custom_call_target="tpu_custom_call" | custom-call | flops 1073741824 | bytes 4194304 | tf_op jit(solution)/shard_map/attend_own/pallas_call | solution.py:203
  75.4 1.9 %collective-permute-start = (bf16[4,4,64,128]{3,2,1,0:T(8,128)(2,1)S(1)}, bf16[4,4,64,128]{3,2,1,0:T(8,128)(2,1)S(1)}, u32[]{:S(2)}, u32[]{:S(2)}) collective-permute-start(bf16[4,4,64,128]{3,2,1,0:T(8,128)(2,1)S(1)} %get-tuple-element.18), channel_id=1, source_target_pairs={{0,112},{8,24},{16,0},{24,40},{32,16},{40,56},{48,32},{56,72},{64,... | collective-permute-start | bytes 786440 | tf_op jit(solution)/shard_map/ppermute | solution.py:215
  77.3 0.0 collective-permute-done.1.refs_0_
  77.3 1.6 %collective-permute-done.2.refs_1_ = bf16[4,4,64,128]{3,2,1,0:T(8,128)(2,1)S(1)} collective-permute-done((bf16[4,4,64,128]{3,2,1,0:T(8,128)(2,1)S(1)}, bf16[4,4,64,128]{3,2,1,0:T(8,128)(2,1)S(1)}, u32[]{:S(2)}, u32[]{:S(2)}) %collective-permute-start.2) | collective-permute-done | bytes 262176 | tf_op jit(solution)/shard_map/ppermute | solution.py:199
  78.9 3.1 %attend_middle.1 = (f32[8,128,256]{2,1,0:T(8,128)S(1)}, f32[8,16,256]{2,1,0:T(8,128)S(1)}) custom-call(s32[40]{0:T(128)S(1)} %copy-done, bf16[256,1024]{1,0:T(8,128)(2,1)S(1)} %copy-done.1, bf16[4,4,64,128]{3,2,1,0:T(8,128)(2,1)S(1)} %collective-permute-done.1.refs_0_, bf16[4,4,64,128]{3,2,1,0:T(8,128)(2,1)S(1)} %collective-permute-done.2.refs_1_, ...), custom_call_target="tpu_custom_call" | custom-call | flops 1073741824 | bytes 4194304 | tf_op jit(solution)/shard_map/attend_middle/pallas_call | solution.py:203
  82.0 4.1 %collective-permute-done.refs_0_ = bf16[4,4,64,128]{3,2,1,0:T(8,128)(2,1)S(1)} collective-permute-done((bf16[4,4,64,128]{3,2,1,0:T(8,128)(2,1)S(1)}, bf16[4,4,64,128]{3,2,1,0:T(8,128)(2,1)S(1)}, u32[]{:S(2)}, u32[]{:S(2)}) %collective-permute-start) | collective-permute-done | bytes 262176 | tf_op jit(solution)/shard_map/ppermute | solution.py:215
  86.1 3.2 %attend_last.1 = bf16[256,1024]{1,0:T(8,128)(2,1)} custom-call(s32[40]{0:T(128)S(1)} %copy-done, bf16[256,1024]{1,0:T(8,128)(2,1)S(1)} %copy-done.1, bf16[4,4,64,128]{3,2,1,0:T(8,128)(2,1)S(1)} %collective-permute-done.refs_0_, f32[8,128,256]{2,1,0:T(8,128)S(1)} %get-tuple-element.21.refs_1_, f32[8,16,256]{2,1,0:T(8,128)S(1)} %get-tuple-element.22.refs_2_), custom_call_target="tpu_custom_call" | custom-call | flops 1073741824 | bytes 4194304 | tf_op jit(solution)/shard_map/attend_last/pallas_call | solution.py:203
  (1 shorter events, 0.0 us)
Async XLA Ops:
  44.4 0.7 copy-start
  60.4 12.7 %copy-start.1 = (bf16[256,1024]{1,0:T(8,128)(2,1)S(1)}, bf16[256,1024]{1,0:T(8,128)(2,1)}, u32[]{:S(2)}) copy-start(bf16[256,1024]{1,0:T(8,128)(2,1)} %queries_ref.5) | copy-start | bytes 1572868
  60.5 16.9 %collective-permute-start.1 = (bf16[4,4,64,128]{3,2,1,0:T(8,128)(2,1)S(1)}, bf16[4,4,64,128]{3,2,1,0:T(8,128)(2,1)S(1)}, u32[]{:S(2)}, u32[]{:S(2)}) collective-permute-start(bf16[4,4,64,128]{3,2,1,0:T(8,128)(2,1)S(1)} %get-tuple-element.23.refs_0_), channel_id=1, source_target_pairs={{0,8},{8,0},{16,24},{24,16},{32,40},{40,32},{48,56},{56,48},{64,72... | collective-permute-start | bytes 786440 | tf_op jit(solution)/shard_map/ppermute | solution.py:198
  66.9 12.1 %collective-permute-start.2 = (bf16[4,4,64,128]{3,2,1,0:T(8,128)(2,1)S(1)}, bf16[4,4,64,128]{3,2,1,0:T(8,128)(2,1)S(1)}, u32[]{:S(2)}, u32[]{:S(2)}) collective-permute-start(bf16[4,4,64,128]{3,2,1,0:T(8,128)(2,1)S(1)} %get-tuple-element.18), channel_id=1, source_target_pairs={{0,120},{8,16},{16,8},{24,32},{32,24},{40,48},{48,40},{56,64},{64,... | collective-permute-start | bytes 786440 | tf_op jit(solution)/shard_map/ppermute | solution.py:199
  75.4 10.7 %collective-permute-start = (bf16[4,4,64,128]{3,2,1,0:T(8,128)(2,1)S(1)}, bf16[4,4,64,128]{3,2,1,0:T(8,128)(2,1)S(1)}, u32[]{:S(2)}, u32[]{:S(2)}) collective-permute-start(bf16[4,4,64,128]{3,2,1,0:T(8,128)(2,1)S(1)} %get-tuple-element.18), channel_id=1, source_target_pairs={{0,112},{8,24},{16,0},{24,40},{32,16},{40,56},{48,32},{56,72},{64,... | collective-permute-start | bytes 786440 | tf_op jit(solution)/shard_map/ppermute | solution.py:215

commit v3 on v2

--- a/solution.py
+++ b/solution.py
@@ -26,11 +26,9 @@
 
 def pack_kernel(parent_ref, owner_ref, lengths_ref, keys_ref, values_ref, out_ref, facts_ref, span_at_ref):
     for kind, ref in enumerate((keys_ref, values_ref)):
-        for strip in range(4):
-            rows = ref[pl.ds(strip * STRIP, STRIP), :]
+        for part in range(2):
             for head in range(HEADS):
-                columns = rows[:, head * HD : (head + 1) * HD]
-                out_ref[kind * 2 + strip // 2, strip % 2, pl.ds(head * STRIP, STRIP), :] = columns
+                out_ref[kind * 2 + part, head] = ref[pl.ds(part * 16, 16), pl.ds(head * HD, HD)]
     half = lax.axis_index("zl")
     pair = lax.axis_index("zb") * 2 + lax.axis_index("i")
     mine = lax.axis_index("x")
@@ -64,7 +62,7 @@
         for side in range(2):
             for level in range(1 + LEVELS):
                 source = facts_ref[TABLE + (x * 2 + side) * (1 + LEVELS) + level]
-                out_ref[x, side, level] = gathered_ref[source]
+                out_ref[x, side, level] = gathered_ref[source >> 1, :, source & 1]
 
 
 def partial_attention(queries, keys, values, causal):
@@ -119,13 +117,13 @@
     own_i = lax.axis_index("i")
     count = facts_ref[0]
     causal = causal_mask(own_i if begins else 1 - own_i) if near_count else None
-    positions = half * HALF + lax.broadcasted_iota(jnp.int32, (HALF, HD), 0)
+    positions = half * HALF + lax.broadcasted_iota(jnp.int32, (1, HALF), 1)
     valid = positions < facts_ref[1]
 
     def finish(head, top, total, summed):
         if ends:
-            result = (summed * (1.0 / total)).T
-            outs[0][:, head * HD : (head + 1) * HD] = jnp.where(valid, result, 0.0).astype(jnp.bfloat16)
+            result = summed * jnp.where(valid, 1.0 / total, 0.0)
+            outs[0][:, head * HD : (head + 1) * HD] = result.astype(jnp.bfloat16).T
         else:
             save(*outs, head, top, total, summed)
 
@@ -174,7 +172,7 @@
     packed, facts = pl.pallas_call(
         pack_kernel,
         out_shape=[
-            jax.ShapeDtypeStruct((4, 2, SHARE, HD), bf16),
+            jax.ShapeDtypeStruct((4, HEADS, 2 * STRIP, HD), bf16),
             jax.ShapeDtypeStruct((TABLE + PLACES * (1 + LEVELS),), jnp.int32),
         ],
         in_specs=[SMEM, SMEM, SMEM, VMEM, VMEM],
@@ -182,17 +180,17 @@
         scratch_shapes=[pltpu.SMEM((SPANS,), jnp.int32)],
         name="pack_heads",
     )(parent, owner, lengths, keys, values)
-    spread = lax.all_to_all(packed.reshape(64, STRIP, HD), ("x", "i", "y", "c"), 0, 0, tiled=True)
-    gathered = lax.all_gather(spread.reshape(PLACES, SHARE, HD), "zb", axis=0, tiled=True)
+    spread = lax.all_to_all(packed.reshape(64, STRIP, HD), ("x", "y", "c", "i"), 0, 0, tiled=True)
+    gathered = lax.all_gather(spread.reshape(4, HEADS, 2, STRIP, HD), "zb", axis=0, tiled=True)
     picked = pl.pallas_call(
         pick_kernel,
-        out_shape=jax.ShapeDtypeStruct((4, 2, 1 + LEVELS, SHARE, HD), bf16),
+        out_shape=jax.ShapeDtypeStruct((4, 2, 1 + LEVELS, HEADS, STRIP, HD), bf16),
         in_specs=[SMEM, VMEM],
         out_specs=VMEM,
         compiler_params=small,
         name="pick_ancestors",
     )(facts, gathered)
-    passed = lax.all_to_all(picked, "x", 0, 0, tiled=True)
+    passed = lax.all_to_all(picked.reshape(4, 2, 1 + LEVELS, SHARE, HD), "x", 0, 0, tiled=True)
     ours, beside = passed[:, 0], passed[:, 1]
     ring = ("zb", "i", "zl")
     far = lax.ppermute(ours, ring, [(z, z ^ 1) for z in range(16)])

time: 89.6 us -> 89.4 us (level)
  the two profiles are of different devices: /device:TPU:72 before, /device:TPU:64 now
where the time goes in v3:
time: 89.4 us; the launch traced here: 89.1 us
  blocking collectives  58 us (65%)
  starting transfers between devices  14.2 us (16%)
  Pallas kernels  10.7 us (12%)
  waiting for transfers between devices  5.37 us (6%)
    all_gather x1, blocking collectives, on_device(): lax.all_gather(spread.reshape(4, HEADS, 2, STRIP, HD), 'zb', axis=0, tile...  30 us
    all_to_all x1, blocking collectives, on_device(): lax.all_to_all(packed.reshape(64, STRIP, HD), ('x', 'y', 'c', 'i'), 0, 0,...  17.3 us
    all_to_all x1, blocking collectives, on_device(): lax.all_to_all(picked.reshape(4, 2, 1 + LEVELS, SHARE, HD), 'x', 0, 0, ti...  10.7 us
    ppermute x1, starting transfers between devices, on_device(): far = lax.ppermute(ours, ring, [(z, z ^ 1) for z in range(16)])  8.76 us
    pallas_call x3, Pallas kernels, attend(): pl.pallas_call(functools.partial(attend_kernel, begins, ends, near_count,...  8.45 us
    ppermute x1, waiting for transfers between devices, on_device(): lax.ppermute(beside, ring, [(z, (z + (2 if z % 2 else -2)) % 16) for z in...  4.29 us
    ppermute x1, starting transfers between devices, on_device(): lax.ppermute(beside, ring, [(z, (z + (1 if z % 2 else -1)) % 16) for z in...  3.5 us
    ppermute x1, starting transfers between devices, on_device(): lax.ppermute(beside, ring, [(z, (z + (2 if z % 2 else -2)) % 16) for z in...  1.92 us
  transfers between devices with their start and end apart: 3, of which 2 were waited for; matrix products, arithmetic and copies ran while one was open for 0% of the time, Pallas kernels for 6%

profile of v3, /device:TPU:64, one launch (start us, length us, event | category | flops | bytes accessed | tf_op | source)
XLA Modules:
  0.0 89.1 jit_solution(655944399884190062)
XLA Ops:
  0.0 1.6 %pack_heads.1 = (bf16[4,8,16,128]{3,2,1,0:T(8,128)(2,1)}, s32[40]{0:T(128)}) custom-call(s32[32]{0:T(128)} %parent_ref.1, s32[32]{0:T(128)} %owner_ref.1, s32[32]{0:T(128)} %lengths_ref.1, bf16[32,1024]{1,0:T(8,128)(2,1)} %keys_ref.1, bf16[32,1024]{1,0:T(8,128)(2,1)} %values_ref.1), custom_call_target="tpu_custom_call" | custom-call | tf_op jit(solution)/shard_map/pack_heads/pallas_call | solution.py:172
  1.6 17.3 %all_to_all.10 = bf16[64,8,128]{2,1,0:T(8,128)(2,1)S(1)} all-to-all(bf16[64,8,128]{2,1,0:T(8,128)(2,1)} %bitcast.13), channel_id=1, replica_groups=mesh['x'=4,'zb'=4,'i'=2,'zl'=2,'y'=4,'c'=2] {'x','y','c','i'}, dimensions={0} | all-to-all | bytes 262144 | tf_op jit(solution)/shard_map/all_to_all | solution.py:183
  18.9 30.0 %all_gather.3.gathered_ref = bf16[16,8,2,8,128]{4,3,2,1,0:T(8,128)(2,1)S(1)} all-gather(bf16[4,8,2,8,128]{4,3,2,1,0:T(8,128)(2,1)S(1)} %bitcast.12), channel_id=1, replica_groups=mesh['x'=4,'zb'=4,'i'=2,'zl'=2,'y'=4,'c'=2] {'zb'}, dimensions={0}, use_global_device_ids=true | all-gather | bytes 655360 | tf_op jit(solution)/shard_map/all_gather | solution.py:184
  48.9 0.0 copy-start
  48.9 0.7 copy-done
  49.6 0.7 pick_ancestors.1
  50.3 10.7 %all_to_all.11 = bf16[4,2,4,64,128]{4,3,2,1,0:T(8,128)(2,1)S(1)} all-to-all(bf16[4,2,4,64,128]{4,3,2,1,0:T(8,128)(2,1)S(1)} %bitcast.11), channel_id=1, replica_groups=mesh['x'=4,'zb'=4,'i'=2,'zl'=2,'y'=4,'c'=2] {'x'}, dimensions={0} | all-to-all | bytes 1048576 | tf_op jit(solution)/shard_map/all_to_all | solution.py:193
  61.0 0.0 copy-start.1
  61.0 8.8 %collective-permute-start.1 = (bf16[4,4,64,128]{3,2,1,0:T(8,128)(2,1)S(1)}, bf16[4,4,64,128]{3,2,1,0:T(8,128)(2,1)S(1)}, u32[]{:S(2)}, u32[]{:S(2)}) collective-permute-start(bf16[4,4,64,128]{3,2,1,0:T(8,128)(2,1)S(1)} %get-tuple-element.23.refs_0_), channel_id=1, source_target_pairs={{0,8},{8,0},{16,24},{24,16},{32,40},{40,32},{48,56},{56,48},{64,72... | collective-permute-start | bytes 786440 | tf_op jit(solution)/shard_map/ppermute | solution.py:196
  69.8 3.5 %collective-permute-start.2 = (bf16[4,4,64,128]{3,2,1,0:T(8,128)(2,1)S(1)}, bf16[4,4,64,128]{3,2,1,0:T(8,128)(2,1)S(1)}, u32[]{:S(2)}, u32[]{:S(2)}) collective-permute-start(bf16[4,4,64,128]{3,2,1,0:T(8,128)(2,1)S(1)} %get-tuple-element.18), channel_id=1, source_target_pairs={{0,120},{8,16},{16,8},{24,32},{32,24},{40,48},{48,40},{56,64},{64,... | collective-permute-start | bytes 786440 | tf_op jit(solution)/shard_map/ppermute | solution.py:197
  73.3 0.0 copy-done.1
  73.3 2.3 %attend_own.1 = (f32[8,128,256]{2,1,0:T(8,128)S(1)}, f32[8,16,256]{2,1,0:T(8,128)S(1)}) custom-call(s32[40]{0:T(128)S(1)} %copy-done, bf16[256,1024]{1,0:T(8,128)(2,1)S(1)} %copy-done.1, bf16[4,4,64,128]{3,2,1,0:T(8,128)(2,1)S(1)} %get-tuple-element.23.refs_0_), custom_call_target="tpu_custom_call" | custom-call | flops 1073741824 | bytes 4194304 | tf_op jit(solution)/shard_map/attend_own/pallas_call | solution.py:201
  75.6 1.9 %collective-permute-start = (bf16[4,4,64,128]{3,2,1,0:T(8,128)(2,1)S(1)}, bf16[4,4,64,128]{3,2,1,0:T(8,128)(2,1)S(1)}, u32[]{:S(2)}, u32[]{:S(2)}) collective-permute-start(bf16[4,4,64,128]{3,2,1,0:T(8,128)(2,1)S(1)} %get-tuple-element.18), channel_id=1, source_target_pairs={{0,112},{8,24},{16,0},{24,40},{32,16},{40,56},{48,32},{56,72},{64,... | collective-permute-start | bytes 786440 | tf_op jit(solution)/shard_map/ppermute | solution.py:213
  77.5 0.0 collective-permute-done.1.refs_0_
  77.5 1.1 %collective-permute-done.2.refs_1_ = bf16[4,4,64,128]{3,2,1,0:T(8,128)(2,1)S(1)} collective-permute-done((bf16[4,4,64,128]{3,2,1,0:T(8,128)(2,1)S(1)}, bf16[4,4,64,128]{3,2,1,0:T(8,128)(2,1)S(1)}, u32[]{:S(2)}, u32[]{:S(2)}) %collective-permute-start.2) | collective-permute-done | bytes 262176 | tf_op jit(solution)/shard_map/ppermute | solution.py:197
  78.6 3.1 %attend_middle.1 = (f32[8,128,256]{2,1,0:T(8,128)S(1)}, f32[8,16,256]{2,1,0:T(8,128)S(1)}) custom-call(s32[40]{0:T(128)S(1)} %copy-done, bf16[256,1024]{1,0:T(8,128)(2,1)S(1)} %copy-done.1, bf16[4,4,64,128]{3,2,1,0:T(8,128)(2,1)S(1)} %collective-permute-done.1.refs_0_, bf16[4,4,64,128]{3,2,1,0:T(8,128)(2,1)S(1)} %collective-permute-done.2.refs_1_, ...), custom_call_target="tpu_custom_call" | custom-call | flops 1073741824 | bytes 4194304 | tf_op jit(solution)/shard_map/attend_middle/pallas_call | solution.py:201
  81.7 4.3 %collective-permute-done.refs_0_ = bf16[4,4,64,128]{3,2,1,0:T(8,128)(2,1)S(1)} collective-permute-done((bf16[4,4,64,128]{3,2,1,0:T(8,128)(2,1)S(1)}, bf16[4,4,64,128]{3,2,1,0:T(8,128)(2,1)S(1)}, u32[]{:S(2)}, u32[]{:S(2)}) %collective-permute-start) | collective-permute-done | bytes 262176 | tf_op jit(solution)/shard_map/ppermute | solution.py:213
  86.0 3.1 %attend_last.1 = bf16[256,1024]{1,0:T(8,128)(2,1)} custom-call(s32[40]{0:T(128)S(1)} %copy-done, bf16[256,1024]{1,0:T(8,128)(2,1)S(1)} %copy-done.1, bf16[4,4,64,128]{3,2,1,0:T(8,128)(2,1)S(1)} %collective-permute-done.refs_0_, f32[8,128,256]{2,1,0:T(8,128)S(1)} %get-tuple-element.21.refs_1_, f32[8,16,256]{2,1,0:T(8,128)S(1)} %get-tuple-element.22.refs_2_), custom_call_target="tpu_custom_call" | custom-call | flops 1073741824 | bytes 4194304 | tf_op jit(solution)/shard_map/attend_last/pallas_call | solution.py:201
  (1 shorter events, 0.0 us)
Async XLA Ops:
  48.9 0.7 copy-start
  61.0 12.3 %copy-start.1 = (bf16[256,1024]{1,0:T(8,128)(2,1)S(1)}, bf16[256,1024]{1,0:T(8,128)(2,1)}, u32[]{:S(2)}) copy-start(bf16[256,1024]{1,0:T(8,128)(2,1)} %queries_ref.5) | copy-start | bytes 1572868
  61.0 16.5 %collective-permute-start.1 = (bf16[4,4,64,128]{3,2,1,0:T(8,128)(2,1)S(1)}, bf16[4,4,64,128]{3,2,1,0:T(8,128)(2,1)S(1)}, u32[]{:S(2)}, u32[]{:S(2)}) collective-permute-start(bf16[4,4,64,128]{3,2,1,0:T(8,128)(2,1)S(1)} %get-tuple-element.23.refs_0_), channel_id=1, source_target_pairs={{0,8},{8,0},{16,24},{24,16},{32,40},{40,32},{48,56},{56,48},{64,72... | collective-permute-start | bytes 786440 | tf_op jit(solution)/shard_map/ppermute | solution.py:196
  69.8 8.8 %collective-permute-start.2 = (bf16[4,4,64,128]{3,2,1,0:T(8,128)(2,1)S(1)}, bf16[4,4,64,128]{3,2,1,0:T(8,128)(2,1)S(1)}, u32[]{:S(2)}, u32[]{:S(2)}) collective-permute-start(bf16[4,4,64,128]{3,2,1,0:T(8,128)(2,1)S(1)} %get-tuple-element.18), channel_id=1, source_target_pairs={{0,120},{8,16},{16,8},{24,32},{32,24},{40,48},{48,40},{56,64},{64,... | collective-permute-start | bytes 786440 | tf_op jit(solution)/shard_map/ppermute | solution.py:197
  75.6 10.4 %collective-permute-start = (bf16[4,4,64,128]{3,2,1,0:T(8,128)(2,1)S(1)}, bf16[4,4,64,128]{3,2,1,0:T(8,128)(2,1)S(1)}, u32[]{:S(2)}, u32[]{:S(2)}) collective-permute-start(bf16[4,4,64,128]{3,2,1,0:T(8,128)(2,1)S(1)} %get-tuple-element.18), channel_id=1, source_target_pairs={{0,112},{8,24},{16,0},{24,40},{32,16},{40,56},{48,32},{56,72},{64,... | collective-permute-start | bytes 786440 | tf_op jit(solution)/shard_map/ppermute | solution.py:213

commit v4 on v3

--- a/solution.py
+++ b/solution.py
@@ -120,10 +120,16 @@
     positions = half * HALF + lax.broadcasted_iota(jnp.int32, (1, HALF), 1)
     valid = positions < facts_ref[1]
 
+    def copy_out(group):
+        columns = pl.ds(group * 2 * HD, 2 * HD)
+        return pltpu.make_async_copy(outs[1].at[:, columns], outs[0].at[:, columns], outs[2].at[group])
+
     def finish(head, top, total, summed):
         if ends:
             result = summed * jnp.where(valid, 1.0 / total, 0.0)
-            outs[0][:, head * HD : (head + 1) * HD] = result.astype(jnp.bfloat16).T
+            outs[1][:, head * HD : (head + 1) * HD] = result.astype(jnp.bfloat16).T
+            if head % 2 == 1:
+                copy_out(head // 2).start()
         else:
             save(*outs, head, top, total, summed)
 
@@ -140,6 +146,7 @@
         if not rows_of(0):
             for head in range(HEADS):
                 finish(head, *stored(head))
+            settle()
             return
         keys, values = (jnp.concatenate(rows_of(kind), axis=0) for kind in range(2))
         parts = partial_attention(head_queries(queries_ref), keys, values, causal)
@@ -152,6 +159,12 @@
             shrink = jnp.exp2((top - newest) * EXP_FACTOR)
             shrink2 = jnp.exp2((top2 - newest) * EXP_FACTOR)
             finish(head, newest, total * shrink + total2 * shrink2, summed * shrink + summed2 * shrink2)
+        settle()
+
+    def settle():
+        if ends:
+            for group in range(HEADS // 2):
+                copy_out(group).wait()
 
     for levels in range(LEVELS + 1):
         if far_count == 0:
@@ -202,7 +215,10 @@
             functools.partial(attend_kernel, begins, ends, near_count, far_count),
             out_shape=jax.ShapeDtypeStruct((HALF, HEADS * HD), bf16) if ends else state,
             in_specs=[SMEM] + [VMEM] * (1 + len(operands)),
-            out_specs=VMEM if ends else [VMEM, VMEM],
+            out_specs=pl.BlockSpec(memory_space=pl.ANY) if ends else [VMEM, VMEM],
+            scratch_shapes=[pltpu.VMEM((HALF, HEADS * HD), bf16), pltpu.SemaphoreType.DMA((HEADS // 2,))]
+            if ends
+            else [],
             compiler_params=params,
             cost_estimate=work,
             name=name,

time: 89.4 us -> 89.5 us (level)
  no operation moved by 1% of the time
where the time goes in v4:
time: 89.5 us; the launch traced here: 89.1 us
  blocking collectives  58 us (65%)
  starting transfers between devices  14.2 us (16%)
  Pallas kernels  10.6 us (12%)
  waiting for transfers between devices  5.37 us (6%)
    all_gather x1, blocking collectives, on_device(): lax.all_gather(spread.reshape(4, HEADS, 2, STRIP, HD), 'zb', axis=0, tile...  30 us
    all_to_all x1, blocking collectives, on_device(): lax.all_to_all(packed.reshape(64, STRIP, HD), ('x', 'y', 'c', 'i'), 0, 0,...  17.3 us
    all_to_all x1, blocking collectives, on_device(): lax.all_to_all(picked.reshape(4, 2, 1 + LEVELS, SHARE, HD), 'x', 0, 0, ti...  10.7 us
    ppermute x1, starting transfers between devices, on_device(): far = lax.ppermute(ours, ring, [(z, z ^ 1) for z in range(16)])  8.76 us
    pallas_call x3, Pallas kernels, attend(): pl.pallas_call(functools.partial(attend_kernel, begins, ends, near_count,...  8.35 us
    ppermute x1, waiting for transfers between devices, on_device(): lax.ppermute(beside, ring, [(z, (z + (2 if z % 2 else -2)) % 16) for z in...  4.29 us
    ppermute x1, starting transfers between devices, on_device(): lax.ppermute(beside, ring, [(z, (z + (1 if z % 2 else -1)) % 16) for z in...  3.5 us
    ppermute x1, starting transfers between devices, on_device(): lax.ppermute(beside, ring, [(z, (z + (2 if z % 2 else -2)) % 16) for z in...  1.92 us
  transfers between devices with their start and end apart: 3, of which 2 were waited for; matrix products, arithmetic and copies ran while one was open for 0% of the time, Pallas kernels for 6%

profile of v4, /device:TPU:64, one launch (start us, length us, event | category | flops | bytes accessed | tf_op | source)
XLA Modules:
  0.0 89.1 jit_solution(17831111018651248523)
XLA Ops:
  0.0 1.6 %pack_heads.1 = (bf16[4,8,16,128]{3,2,1,0:T(8,128)(2,1)}, s32[40]{0:T(128)}) custom-call(s32[32]{0:T(128)} %parent_ref.1, s32[32]{0:T(128)} %owner_ref.1, s32[32]{0:T(128)} %lengths_ref.1, bf16[32,1024]{1,0:T(8,128)(2,1)} %keys_ref.1, bf16[32,1024]{1,0:T(8,128)(2,1)} %values_ref.1), custom_call_target="tpu_custom_call" | custom-call | tf_op jit(solution)/shard_map/pack_heads/pallas_call | solution.py:185
  1.6 17.3 %all_to_all.10 = bf16[64,8,128]{2,1,0:T(8,128)(2,1)S(1)} all-to-all(bf16[64,8,128]{2,1,0:T(8,128)(2,1)} %bitcast.13), channel_id=1, replica_groups=mesh['x'=4,'zb'=4,'i'=2,'zl'=2,'y'=4,'c'=2] {'x','y','c','i'}, dimensions={0} | all-to-all | bytes 262144 | tf_op jit(solution)/shard_map/all_to_all | solution.py:196
  18.9 30.0 %all_gather.3.gathered_ref = bf16[16,8,2,8,128]{4,3,2,1,0:T(8,128)(2,1)S(1)} all-gather(bf16[4,8,2,8,128]{4,3,2,1,0:T(8,128)(2,1)S(1)} %bitcast.12), channel_id=1, replica_groups=mesh['x'=4,'zb'=4,'i'=2,'zl'=2,'y'=4,'c'=2] {'zb'}, dimensions={0}, use_global_device_ids=true | all-gather | bytes 655360 | tf_op jit(solution)/shard_map/all_gather | solution.py:197
  48.9 0.0 copy-start
  48.9 0.7 copy-done
  49.6 0.7 pick_ancestors.1
  50.3 10.7 %all_to_all.11 = bf16[4,2,4,64,128]{4,3,2,1,0:T(8,128)(2,1)S(1)} all-to-all(bf16[4,2,4,64,128]{4,3,2,1,0:T(8,128)(2,1)S(1)} %bitcast.11), channel_id=1, replica_groups=mesh['x'=4,'zb'=4,'i'=2,'zl'=2,'y'=4,'c'=2] {'x'}, dimensions={0} | all-to-all | bytes 1048576 | tf_op jit(solution)/shard_map/all_to_all | solution.py:206
  61.0 0.0 copy-start.1
  61.0 8.8 %collective-permute-start.1 = (bf16[4,4,64,128]{3,2,1,0:T(8,128)(2,1)S(1)}, bf16[4,4,64,128]{3,2,1,0:T(8,128)(2,1)S(1)}, u32[]{:S(2)}, u32[]{:S(2)}) collective-permute-start(bf16[4,4,64,128]{3,2,1,0:T(8,128)(2,1)S(1)} %get-tuple-element.23.refs_0_), channel_id=1, source_target_pairs={{0,8},{8,0},{16,24},{24,16},{32,40},{40,32},{48,56},{56,48},{64,72... | collective-permute-start | bytes 786440 | tf_op jit(solution)/shard_map/ppermute | solution.py:209
  69.8 3.5 %collective-permute-start.2 = (bf16[4,4,64,128]{3,2,1,0:T(8,128)(2,1)S(1)}, bf16[4,4,64,128]{3,2,1,0:T(8,128)(2,1)S(1)}, u32[]{:S(2)}, u32[]{:S(2)}) collective-permute-start(bf16[4,4,64,128]{3,2,1,0:T(8,128)(2,1)S(1)} %get-tuple-element.18), channel_id=1, source_target_pairs={{0,120},{8,16},{16,8},{24,32},{32,24},{40,48},{48,40},{56,64},{64,... | collective-permute-start | bytes 786440 | tf_op jit(solution)/shard_map/ppermute | solution.py:210
  73.3 0.0 copy-done.1
  73.3 2.3 %attend_own.1 = (f32[8,128,256]{2,1,0:T(8,128)S(1)}, f32[8,16,256]{2,1,0:T(8,128)S(1)}) custom-call(s32[40]{0:T(128)S(1)} %copy-done, bf16[256,1024]{1,0:T(8,128)(2,1)S(1)} %copy-done.1, bf16[4,4,64,128]{3,2,1,0:T(8,128)(2,1)S(1)} %get-tuple-element.23.refs_0_), custom_call_target="tpu_custom_call" | custom-call | flops 1073741824 | bytes 4194304 | tf_op jit(solution)/shard_map/attend_own/pallas_call | solution.py:214
  75.6 1.9 %collective-permute-start = (bf16[4,4,64,128]{3,2,1,0:T(8,128)(2,1)S(1)}, bf16[4,4,64,128]{3,2,1,0:T(8,128)(2,1)S(1)}, u32[]{:S(2)}, u32[]{:S(2)}) collective-permute-start(bf16[4,4,64,128]{3,2,1,0:T(8,128)(2,1)S(1)} %get-tuple-element.18), channel_id=1, source_target_pairs={{0,112},{8,24},{16,0},{24,40},{32,16},{40,56},{48,32},{56,72},{64,... | collective-permute-start | bytes 786440 | tf_op jit(solution)/shard_map/ppermute | solution.py:229
  77.5 0.0 collective-permute-done.1.refs_0_
  77.5 1.1 %collective-permute-done.2.refs_1_ = bf16[4,4,64,128]{3,2,1,0:T(8,128)(2,1)S(1)} collective-permute-done((bf16[4,4,64,128]{3,2,1,0:T(8,128)(2,1)S(1)}, bf16[4,4,64,128]{3,2,1,0:T(8,128)(2,1)S(1)}, u32[]{:S(2)}, u32[]{:S(2)}) %collective-permute-start.2) | collective-permute-done | bytes 262176 | tf_op jit(solution)/shard_map/ppermute | solution.py:210
  78.6 3.1 %attend_middle.1 = (f32[8,128,256]{2,1,0:T(8,128)S(1)}, f32[8,16,256]{2,1,0:T(8,128)S(1)}) custom-call(s32[40]{0:T(128)S(1)} %copy-done, bf16[256,1024]{1,0:T(8,128)(2,1)S(1)} %copy-done.1, bf16[4,4,64,128]{3,2,1,0:T(8,128)(2,1)S(1)} %collective-permute-done.1.refs_0_, bf16[4,4,64,128]{3,2,1,0:T(8,128)(2,1)S(1)} %collective-permute-done.2.refs_1_, ...), custom_call_target="tpu_custom_call" | custom-call | flops 1073741824 | bytes 4194304 | tf_op jit(solution)/shard_map/attend_middle/pallas_call | solution.py:214
  81.7 4.3 %collective-permute-done.refs_0_ = bf16[4,4,64,128]{3,2,1,0:T(8,128)(2,1)S(1)} collective-permute-done((bf16[4,4,64,128]{3,2,1,0:T(8,128)(2,1)S(1)}, bf16[4,4,64,128]{3,2,1,0:T(8,128)(2,1)S(1)}, u32[]{:S(2)}, u32[]{:S(2)}) %collective-permute-start) | collective-permute-done | bytes 262176 | tf_op jit(solution)/shard_map/ppermute | solution.py:229
  86.0 3.0 %attend_last.1 = bf16[256,1024]{1,0:T(8,128)(2,1)} custom-call(s32[40]{0:T(128)S(1)} %copy-done, bf16[256,1024]{1,0:T(8,128)(2,1)S(1)} %copy-done.1, bf16[4,4,64,128]{3,2,1,0:T(8,128)(2,1)S(1)} %collective-permute-done.refs_0_, f32[8,128,256]{2,1,0:T(8,128)S(1)} %get-tuple-element.21.refs_1_, f32[8,16,256]{2,1,0:T(8,128)S(1)} %get-tuple-element.22.refs_2_), custom_call_target="tpu_custom_call" | custom-call | flops 1073741824 | bytes 4194304 | tf_op jit(solution)/shard_map/attend_last/pallas_call | solution.py:214
  (1 shorter events, 0.0 us)
Async XLA Ops:
  48.9 0.7 copy-start
  61.0 12.3 %copy-start.1 = (bf16[256,1024]{1,0:T(8,128)(2,1)S(1)}, bf16[256,1024]{1,0:T(8,128)(2,1)}, u32[]{:S(2)}) copy-start(bf16[256,1024]{1,0:T(8,128)(2,1)} %queries_ref.5) | copy-start | bytes 1572868
  61.0 16.5 %collective-permute-start.1 = (bf16[4,4,64,128]{3,2,1,0:T(8,128)(2,1)S(1)}, bf16[4,4,64,128]{3,2,1,0:T(8,128)(2,1)S(1)}, u32[]{:S(2)}, u32[]{:S(2)}) collective-permute-start(bf16[4,4,64,128]{3,2,1,0:T(8,128)(2,1)S(1)} %get-tuple-element.23.refs_0_), channel_id=1, source_target_pairs={{0,8},{8,0},{16,24},{24,16},{32,40},{40,32},{48,56},{56,48},{64,72... | collective-permute-start | bytes 786440 | tf_op jit(solution)/shard_map/ppermute | solution.py:209
  69.8 8.8 %collective-permute-start.2 = (bf16[4,4,64,128]{3,2,1,0:T(8,128)(2,1)S(1)}, bf16[4,4,64,128]{3,2,1,0:T(8,128)(2,1)S(1)}, u32[]{:S(2)}, u32[]{:S(2)}) collective-permute-start(bf16[4,4,64,128]{3,2,1,0:T(8,128)(2,1)S(1)} %get-tuple-element.18), channel_id=1, source_target_pairs={{0,120},{8,16},{16,8},{24,32},{32,24},{40,48},{48,40},{56,64},{64,... | collective-permute-start | bytes 786440 | tf_op jit(solution)/shard_map/ppermute | solution.py:210
  75.6 10.4 %collective-permute-start = (bf16[4,4,64,128]{3,2,1,0:T(8,128)(2,1)S(1)}, bf16[4,4,64,128]{3,2,1,0:T(8,128)(2,1)S(1)}, u32[]{:S(2)}, u32[]{:S(2)}) collective-permute-start(bf16[4,4,64,128]{3,2,1,0:T(8,128)(2,1)S(1)} %get-tuple-element.18), channel_id=1, source_target_pairs={{0,112},{8,24},{16,0},{24,40},{32,16},{40,56},{48,32},{56,72},{64,... | collective-permute-start | bytes 786440 | tf_op jit(solution)/shard_map/ppermute | solution.py:229

commit v5 on v3

--- a/solution.py
+++ b/solution.py
@@ -209,7 +209,7 @@
         )(facts, queries, *operands)
 
     running = attend("attend_own", True, False, 1, 0, ours)
-    beside, running = lax.optimization_barrier((beside, running))
+
     near = lax.ppermute(beside, ring, [(z, (z + (2 if z % 2 else -2)) % 16) for z in range(16)])
     running = attend("attend_middle", False, False, 0, 2, far, further, *running)
     return attend("attend_last", False, True, 1, 0, near, *running)

time: 89.4 us -> 89.4 us (level)
  the two profiles are of different devices: /device:TPU:64 before, /device:TPU:32 now
where the time goes in v5:
time: 89.4 us; the launch traced here: 88.8 us
  blocking collectives  62.1 us (69%)
  starting transfers between devices  12 us (13%)
  Pallas kernels  8.83 us (10%)
  waiting for transfers between devices  5.05 us (6%)
    all_gather x1, blocking collectives, on_device(): lax.all_gather(spread.reshape(4, HEADS, 2, STRIP, HD), 'zb', axis=0, tile...  30.3 us
    all_to_all x1, blocking collectives, on_device(): lax.all_to_all(packed.reshape(64, STRIP, HD), ('x', 'y', 'c', 'i'), 0, 0,...  20.1 us
    all_to_all x1, blocking collectives, on_device(): lax.all_to_all(picked.reshape(4, 2, 1 + LEVELS, SHARE, HD), 'x', 0, 0, ti...  11.8 us
    pallas_call x3, Pallas kernels, attend(): pl.pallas_call(functools.partial(attend_kernel, begins, ends, near_count,...  6.54 us
    ppermute x1, starting transfers between devices, on_device(): far = lax.ppermute(ours, ring, [(z, z ^ 1) for z in range(16)])  6.1 us
    ppermute x1, waiting for transfers between devices, on_device(): lax.ppermute(beside, ring, [(z, (z + (1 if z % 2 else -1)) % 16) for z in...  3.66 us
    ppermute x1, starting transfers between devices, on_device(): lax.ppermute(beside, ring, [(z, (z + (2 if z % 2 else -2)) % 16) for z in...  3.51 us
    ppermute x1, starting transfers between devices, on_device(): lax.ppermute(beside, ring, [(z, (z + (1 if z % 2 else -1)) % 16) for z in...  2.34 us
  transfers between devices with their start and end apart: 3, of which 2 were waited for; matrix products, arithmetic and copies ran while one was open for 0% of the time, Pallas kernels for 4%

profile of v5, /device:TPU:32, one launch (start us, length us, event | category | flops | bytes accessed | tf_op | source)
XLA Modules:
  0.0 88.8 jit_solution(10873849698054571796)
XLA Ops:
  0.0 1.6 %pack_heads.1 = (bf16[4,8,16,128]{3,2,1,0:T(8,128)(2,1)}, s32[40]{0:T(128)}) custom-call(s32[32]{0:T(128)} %parent_ref.1, s32[32]{0:T(128)} %owner_ref.1, s32[32]{0:T(128)} %lengths_ref.1, bf16[32,1024]{1,0:T(8,128)(2,1)} %keys_ref.1, bf16[32,1024]{1,0:T(8,128)(2,1)} %values_ref.1), custom_call_target="tpu_custom_call" | custom-call | tf_op jit(solution)/shard_map/pack_heads/pallas_call | solution.py:172
  1.6 20.1 %all_to_all.10 = bf16[64,8,128]{2,1,0:T(8,128)(2,1)S(1)} all-to-all(bf16[64,8,128]{2,1,0:T(8,128)(2,1)} %bitcast.13), channel_id=1, replica_groups=mesh['x'=4,'zb'=4,'i'=2,'zl'=2,'y'=4,'c'=2] {'x','y','c','i'}, dimensions={0} | all-to-all | bytes 262144 | tf_op jit(solution)/shard_map/all_to_all | solution.py:183
  21.7 30.3 %all_gather.3.gathered_ref = bf16[16,8,2,8,128]{4,3,2,1,0:T(8,128)(2,1)S(1)} all-gather(bf16[4,8,2,8,128]{4,3,2,1,0:T(8,128)(2,1)S(1)} %bitcast.12), channel_id=1, replica_groups=mesh['x'=4,'zb'=4,'i'=2,'zl'=2,'y'=4,'c'=2] {'zb'}, dimensions={0}, use_global_device_ids=true | all-gather | bytes 655360 | tf_op jit(solution)/shard_map/all_gather | solution.py:184
  52.0 0.0 copy-start
  52.0 0.7 copy-done
  52.7 0.7 pick_ancestors.1
  53.4 11.8 %all_to_all.11 = bf16[4,2,4,64,128]{4,3,2,1,0:T(8,128)(2,1)S(1)} all-to-all(bf16[4,2,4,64,128]{4,3,2,1,0:T(8,128)(2,1)S(1)} %bitcast.11), channel_id=1, replica_groups=mesh['x'=4,'zb'=4,'i'=2,'zl'=2,'y'=4,'c'=2] {'x'}, dimensions={0} | all-to-all | bytes 1048576 | tf_op jit(solution)/shard_map/all_to_all | solution.py:193
  65.1 0.0 copy-start.1
  65.2 6.1 %collective-permute-start.1 = (bf16[4,4,64,128]{3,2,1,0:T(8,128)(2,1)S(1)}, bf16[4,4,64,128]{3,2,1,0:T(8,128)(2,1)S(1)}, u32[]{:S(2)}, u32[]{:S(2)}) collective-permute-start(bf16[4,4,64,128]{3,2,1,0:T(8,128)(2,1)S(1)} %get-tuple-element.17.refs_0_), channel_id=1, source_target_pairs={{0,8},{8,0},{16,24},{24,16},{32,40},{40,32},{48,56},{56,48},{64,72... | collective-permute-start | bytes 786440 | tf_op jit(solution)/shard_map/ppermute | solution.py:196
  71.3 2.3 %collective-permute-start.2 = (bf16[4,4,64,128]{3,2,1,0:T(8,128)(2,1)S(1)}, bf16[4,4,64,128]{3,2,1,0:T(8,128)(2,1)S(1)}, u32[]{:S(2)}, u32[]{:S(2)}) collective-permute-start(bf16[4,4,64,128]{3,2,1,0:T(8,128)(2,1)S(1)} %get-tuple-element.18), channel_id=1, source_target_pairs={{0,120},{8,16},{16,8},{24,32},{32,24},{40,48},{48,40},{56,64},{64,... | collective-permute-start | bytes 786440 | tf_op jit(solution)/shard_map/ppermute | solution.py:197
  73.6 3.5 %collective-permute-start = (bf16[4,4,64,128]{3,2,1,0:T(8,128)(2,1)S(1)}, bf16[4,4,64,128]{3,2,1,0:T(8,128)(2,1)S(1)}, u32[]{:S(2)}, u32[]{:S(2)}) collective-permute-start(bf16[4,4,64,128]{3,2,1,0:T(8,128)(2,1)S(1)} %get-tuple-element.18), channel_id=1, source_target_pairs={{0,112},{8,24},{16,0},{24,40},{32,16},{40,56},{48,32},{56,72},{64,... | collective-permute-start | bytes 786440 | tf_op jit(solution)/shard_map/ppermute | solution.py:213
  77.1 0.0 copy-done.1
  77.1 1.6 %attend_own.1 = (f32[8,128,256]{2,1,0:T(8,128)S(1)}, f32[8,16,256]{2,1,0:T(8,128)S(1)}) custom-call(s32[40]{0:T(128)S(1)} %copy-done, bf16[256,1024]{1,0:T(8,128)(2,1)S(1)} %copy-done.1, bf16[4,4,64,128]{3,2,1,0:T(8,128)(2,1)S(1)} %get-tuple-element.17.refs_0_), custom_call_target="tpu_custom_call" | custom-call | flops 1073741824 | bytes 4194304 | tf_op jit(solution)/shard_map/attend_own/pallas_call | solution.py:201
  78.7 0.0 collective-permute-done.1.refs_0_
  78.7 3.7 %collective-permute-done.2.refs_1_ = bf16[4,4,64,128]{3,2,1,0:T(8,128)(2,1)S(1)} collective-permute-done((bf16[4,4,64,128]{3,2,1,0:T(8,128)(2,1)S(1)}, bf16[4,4,64,128]{3,2,1,0:T(8,128)(2,1)S(1)}, u32[]{:S(2)}, u32[]{:S(2)}) %collective-permute-start.2) | collective-permute-done | bytes 262176 | tf_op jit(solution)/shard_map/ppermute | solution.py:197
  82.4 2.4 %attend_middle.1 = (f32[8,128,256]{2,1,0:T(8,128)S(1)}, f32[8,16,256]{2,1,0:T(8,128)S(1)}) custom-call(s32[40]{0:T(128)S(1)} %copy-done, bf16[256,1024]{1,0:T(8,128)(2,1)S(1)} %copy-done.1, bf16[4,4,64,128]{3,2,1,0:T(8,128)(2,1)S(1)} %collective-permute-done.1.refs_0_, bf16[4,4,64,128]{3,2,1,0:T(8,128)(2,1)S(1)} %collective-permute-done.2.refs_1_, ...), custom_call_target="tpu_custom_call" | custom-call | flops 1073741824 | bytes 4194304 | tf_op jit(solution)/shard_map/attend_middle/pallas_call | solution.py:201
  84.8 1.4 %collective-permute-done.refs_0_ = bf16[4,4,64,128]{3,2,1,0:T(8,128)(2,1)S(1)} collective-permute-done((bf16[4,4,64,128]{3,2,1,0:T(8,128)(2,1)S(1)}, bf16[4,4,64,128]{3,2,1,0:T(8,128)(2,1)S(1)}, u32[]{:S(2)}, u32[]{:S(2)}) %collective-permute-start) | collective-permute-done | bytes 262176 | tf_op jit(solution)/shard_map/ppermute | solution.py:213
  86.2 2.5 %attend_last.1 = bf16[256,1024]{1,0:T(8,128)(2,1)} custom-call(s32[40]{0:T(128)S(1)} %copy-done, bf16[256,1024]{1,0:T(8,128)(2,1)S(1)} %copy-done.1, bf16[4,4,64,128]{3,2,1,0:T(8,128)(2,1)S(1)} %collective-permute-done.refs_0_, f32[8,128,256]{2,1,0:T(8,128)S(1)} %get-tuple-element.15.refs_1_, f32[8,16,256]{2,1,0:T(8,128)S(1)} %get-tuple-element.16.refs_2_), custom_call_target="tpu_custom_call" | custom-call | flops 1073741824 | bytes 4194304 | tf_op jit(solution)/shard_map/attend_last/pallas_call | solution.py:201
  (1 shorter events, 0.0 us)
Async XLA Ops:
  52.0 0.7 copy-start
  65.1 12.0 %copy-start.1 = (bf16[256,1024]{1,0:T(8,128)(2,1)S(1)}, bf16[256,1024]{1,0:T(8,128)(2,1)}, u32[]{:S(2)}) copy-start(bf16[256,1024]{1,0:T(8,128)(2,1)} %queries_ref.5) | copy-start | bytes 1572868
  65.2 13.6 %collective-permute-start.1 = (bf16[4,4,64,128]{3,2,1,0:T(8,128)(2,1)S(1)}, bf16[4,4,64,128]{3,2,1,0:T(8,128)(2,1)S(1)}, u32[]{:S(2)}, u32[]{:S(2)}) collective-permute-start(bf16[4,4,64,128]{3,2,1,0:T(8,128)(2,1)S(1)} %get-tuple-element.17.refs_0_), channel_id=1, source_target_pairs={{0,8},{8,0},{16,24},{24,16},{32,40},{40,32},{48,56},{56,48},{64,72... | collective-permute-start | bytes 786440 | tf_op jit(solution)/shard_map/ppermute | solution.py:196
  71.3 11.1 %collective-permute-start.2 = (bf16[4,4,64,128]{3,2,1,0:T(8,128)(2,1)S(1)}, bf16[4,4,64,128]{3,2,1,0:T(8,128)(2,1)S(1)}, u32[]{:S(2)}, u32[]{:S(2)}) collective-permute-start(bf16[4,4,64,128]{3,2,1,0:T(8,128)(2,1)S(1)} %get-tuple-element.18), channel_id=1, source_target_pairs={{0,120},{8,16},{16,8},{24,32},{32,24},{40,48},{48,40},{56,64},{64,... | collective-permute-start | bytes 786440 | tf_op jit(solution)/shard_map/ppermute | solution.py:197
  73.6 12.6 %collective-permute-start = (bf16[4,4,64,128]{3,2,1,0:T(8,128)(2,1)S(1)}, bf16[4,4,64,128]{3,2,1,0:T(8,128)(2,1)S(1)}, u32[]{:S(2)}, u32[]{:S(2)}) collective-permute-start(bf16[4,4,64,128]{3,2,1,0:T(8,128)(2,1)S(1)} %get-tuple-element.18), channel_id=1, source_target_pairs={{0,112},{8,24},{16,0},{24,40},{32,16},{40,56},{48,32},{56,72},{64,... | collective-permute-start | bytes 786440 | tf_op jit(solution)/shard_map/ppermute | solution.py:213
